TPU v7x, 256 devices: a whole 4x4x8 slice. The times are simulated.
256 devices in a mesh: dp: 32 (over z, x), seq: 8 (over y, core).
Axes of the slice: x: 4, y: 4, z: 8, core: 2. Of those that a mesh axis runs over, the one named last changes fastest.
Arguments:
- patches: bfloat16 [32, 98304], P(None, ('dp', 'seq')), may hold values from -12 to 12
- segment_ids: int32 [32, 3072], P('dp'), may hold values from 0 to 15, never falling along the last dimension, each value on 1 to 2304 neighbouring positions
- regroup_plan: int32 [32, 5, 64], P('dp'), may hold values from 0 to 383, as said below
- input_weight: bfloat16 [32, 1280], replicated, may hold values from -1 to 1
- input_bias: float32 [1280], replicated, may hold values from -3 to 3
- skip_weight: bfloat16 [32, 1280], replicated, may hold values from -1 to 1
- hidden_weight: bfloat16 [1280, 1280], replicated, may hold values from -0.15625 to 0.15625
- output_bias: float32 [1280], replicated, may hold values from -3 to 3
- norm_gain: float32 [1280], replicated, may hold values from 0.1 to 1.9
- head_scale: float32 [8], replicated, may hold values from 1 to 4
- qkv_weight: bfloat16 [1280, 3, 640], replicated, may hold values from -0.15625 to 0.15625
- out_weight: bfloat16 [640, 1280], P(None, ('dp', 'seq')), may hold values from -0.25 to 0.25
- cotangent: bfloat16 [98304, 1280], P(('dp', 'seq')), may hold values from -0.3125 to 0.3125
Outputs:
- layer_out: bfloat16 [98304, 1280], P(('dp', 'seq'))
- out_grad: float32 [640, 1280], P(None, ('dp', 'seq'))
Inputs may be any that keep to these rules, and one draw needn't show every extreme that they name: `regroup_plan`: piece s * 8 + d of a window moves rows of source shard s to destination shard d: one piece for each pair, each moving one row or more. The pieces of a window cover each of the 384 rows of every source shard once and each of the 384 rows of every destination shard once. A piece moves at most 96 rows, and in every window some piece moves exactly 96. `segment_ids`: series ids never fall along a window's positions; one series of each window has exactly 2304 positions.
All inputs are finite; a program needn't handle non-finite values.
Results may differ from a plain program's by a relative error of at most 0.015.
Values may be sent and summed in bfloat16 or wider, within the bound.
A program may use at most 64 MiB of HBM per device.

v0:
```python
import math
import jax
import jax.numpy as jnp
from jax import lax
from jax.sharding import PartitionSpec as P

HD = 80
EPSILON = 1e-06
CONTRACT_FIRST = (((0,), (0,)), ((), ()))


def row_norm(values):
    return values * lax.rsqrt(jnp.mean(values * values, axis=-1, keepdims=True) + EPSILON)


def place_table(plan_rows, shard_rows, shard_count):
    source = plan_rows[0]
    first_row = plan_rows[1]
    row_count = plan_rows[2]
    target = plan_rows[3]
    offset_row = plan_rows[4]
    window_len = shard_rows * shard_count
    loader_row = jnp.arange(window_len, dtype=jnp.int32)
    begin_row = source * shard_rows + first_row
    inside = (loader_row[None, :] >= begin_row[:, None]) & (
        loader_row[None, :] < (begin_row + row_count)[:, None]
    )
    earlier = (
        (source[:, None] == source[None, :])
        & (target[:, None] == target[None, :])
        & (first_row[None, :] < first_row[:, None])
    )
    base_rank = jnp.sum(jnp.where(earlier, row_count[None, :], 0), axis=1)
    position = jnp.sum(
        jnp.where(
            inside, (target * shard_rows + offset_row - begin_row)[:, None] + loader_row[None, :], 0
        ),
        axis=0,
    )
    slot_rank = jnp.sum(
        jnp.where(inside, (base_rank - begin_row)[:, None] + loader_row[None, :], 0), axis=0
    )
    return (position, slot_rank)


def patch_block(columns, input_weight, input_bias, skip_weight, hidden_weight, output_bias):
    pre_act = (
        lax.dot_general(columns, input_weight, CONTRACT_FIRST, preferred_element_type=jnp.float32)
        + input_bias
    )
    hidden = jax.nn.silu(pre_act).astype(jnp.bfloat16)
    skipped = lax.dot_general(
        columns, skip_weight, CONTRACT_FIRST, preferred_element_type=jnp.float32
    )
    embedded = (
        jnp.dot(hidden, hidden_weight, preferred_element_type=jnp.float32) + skipped + output_bias
    )
    return embedded.astype(jnp.bfloat16)


def per_device(
    patches,
    segment_ids,
    regroup_plan,
    input_weight,
    input_bias,
    skip_weight,
    hidden_weight,
    output_bias,
    norm_gain,
    head_scale,
    qkv_weight,
    out_weight,
    cotangent,
):
    shard_count = lax.axis_size("seq")
    shard_index = lax.axis_index("seq")
    shard_rows = cotangent.shape[0]
    model_width = cotangent.shape[1]
    window_len = shard_rows * shard_count
    capacity = 2 * shard_rows // shard_count
    position, slot_rank = place_table(regroup_plan[0], shard_rows, shard_count)
    loader_row = jnp.arange(window_len, dtype=jnp.int32)
    own_rows = lax.dynamic_slice_in_dim(position, shard_index * shard_rows, shard_rows, 0)
    own_ranks = lax.dynamic_slice_in_dim(slot_rank, shard_index * shard_rows, shard_rows, 0)
    send_slot = own_rows // shard_rows * capacity + own_ranks
    send_table = (
        jnp.full((shard_count * capacity,), shard_rows, jnp.int32)
        .at[send_slot]
        .set(jnp.arange(shard_rows, dtype=jnp.int32))
    )
    landing = jnp.where(position // shard_rows == shard_index, position % shard_rows, shard_rows)
    receive_table = (
        jnp.zeros((shard_rows,), jnp.int32)
        .at[landing]
        .set(loader_row // shard_rows * capacity + slot_rank, mode="drop")
    )
    local_embed = patch_block(
        patches, input_weight, input_bias, skip_weight, hidden_weight, output_bias
    )
    padded = jnp.concatenate([local_embed, jnp.zeros((1, model_width), jnp.bfloat16)], axis=0)
    arrived = lax.all_to_all(padded[send_table], "seq", split_axis=0, concat_axis=0, tiled=True)
    embedded = arrived[receive_table]
    normed = (row_norm(embedded.astype(jnp.float32)) * norm_gain).astype(jnp.bfloat16)
    projected = jnp.dot(
        normed, qkv_weight.reshape(model_width, -1), preferred_element_type=jnp.float32
    )
    projected = projected.astype(jnp.bfloat16).reshape(shard_rows, 3, -1)
    head_rows = lax.all_to_all(projected, "seq", split_axis=2, concat_axis=0, tiled=True)
    local_width = head_rows.shape[2]
    local_heads = local_width // HD
    queries = row_norm(
        head_rows[:, 0].reshape(window_len, local_heads, HD).astype(jnp.float32)
    ).astype(jnp.bfloat16)
    key_rows = row_norm(
        head_rows[:, 1].reshape(window_len, local_heads, HD).astype(jnp.float32)
    ).astype(jnp.bfloat16)
    value_rows = head_rows[:, 2].reshape(window_len, local_heads, HD)
    factor = lax.dynamic_slice_in_dim(head_scale, shard_index * local_heads, local_heads, 0) * (
        1.0 / math.sqrt(HD)
    )
    segment_row = segment_ids[0]
    block_len = min(512, window_len)
    block_count = window_len // block_len
    pieces = []
    for block_index in range(block_count):
        query_first = block_index * block_len
        query_part = queries[query_first : query_first + block_len]
        query_pos = query_first + jnp.arange(block_len, dtype=jnp.int32)
        query_seg = segment_row[query_first : query_first + block_len]
        key_len = query_first + block_len
        key_part = lax.slice_in_dim(key_rows, 0, key_len, axis=0)
        value_part = lax.slice_in_dim(value_rows, 0, key_len, axis=0)
        key_seg = lax.slice_in_dim(segment_row, 0, key_len, axis=0)
        key_pos = jnp.arange(key_len, dtype=jnp.int32)
        scores = (
            jnp.einsum("qhd,khd->hqk", query_part, key_part, preferred_element_type=jnp.float32)
            * factor[:, None, None]
        )
        allowed = (query_seg[:, None] == key_seg[None, :]) & (
            key_pos[None, :] <= query_pos[:, None]
        )
        weights = jnp.where(allowed[None], jnp.exp(scores), 0.0)
        summed = jnp.einsum(
            "hqk,khd->qhd",
            weights.astype(jnp.bfloat16),
            value_part,
            preferred_element_type=jnp.float32,
        )
        summed, denominator = (summed, jnp.sum(weights, axis=-1))
        pieces.append(
            (summed / jnp.transpose(denominator)[:, :, None]).reshape(block_len, local_width)
        )
    attended = jnp.concatenate(pieces, axis=0).astype(jnp.bfloat16)
    returned = lax.all_to_all(attended, "seq", split_axis=0, concat_axis=1, tiled=True)
    branch = jnp.dot(
        returned,
        lax.all_gather(out_weight, ("dp", "seq"), axis=1, tiled=True),
        preferred_element_type=jnp.float32,
    )
    layer_out = (embedded.astype(jnp.float32) + branch).astype(jnp.bfloat16)
    grad_term = lax.dot_general(
        returned, cotangent, CONTRACT_FIRST, preferred_element_type=jnp.float32
    )
    out_grad = lax.psum_scatter(grad_term, ("dp", "seq"), scatter_dimension=1, tiled=True)
    return (layer_out, out_grad)


def solution(mesh):
    placed = (
        P(None, ("dp", "seq")),
        P("dp", None),
        P("dp", None, None),
        P(),
        P(),
        P(),
        P(),
        P(),
        P(),
        P(),
        P(),
        P(None, ("dp", "seq")),
        P(("dp", "seq"), None),
    )
    return jax.shard_map(
        per_device,
        mesh=mesh,
        in_specs=placed,
        out_specs=(P(("dp", "seq"), None), P(None, ("dp", "seq"))),
        check_vma=False,
    )
```

profile of v0, /device:TPU:2, one launch (start us, length us, event | category | flops | bytes accessed | tf_op | source)
XLA Modules:
  0.0 472.5 jit_solution(12129723158445891963)
XLA Ops:
  7.2 0.9 slice_bitcast_fusion.37
  10.1 2.9 scatter_custom_fusion
  13.1 4.2 fusion.23
  17.3 2.0 fusion.9
  19.3 1.0 concatenate.7
  20.3 6.5 %gather_fusion = bf16[768,1280]{1,0:T(8,128)(2,1)} fusion(bf16[385,1280]{1,0:T(8,128)(2,1)} %concatenate.7, s32[1024]{0:T(1024)S(1)} %pad_clamp_fusion.1), kind=kCustom, calls=%fused_computation | custom fusion | bytes 3935232 | tf_op jit(solution)/shard_map/gather | solution.py:102
  26.8 4.5 all-to-all-start
  31.3 8.2 %copy.25 = bf16[1280,3,640]{0,2,1:T(8,128)(2,1)} copy(bf16[1280,3,640]{2,0,1:T(8,128)(2,1)} %param.23) | data formatting | bytes 9830400 | tf_op args[10]
  39.6 11.9 %scatter_custom_fusion.1 = s32[384]{0:T(512)S(1)} fusion(s32[3072]{0:T(1024)S(1)} %bitcast.265, s32[3072]{0:T(1024)S(1)} %get-tuple-element.36, s32[]{:T(128)} %constant.25.clone.1), kind=kCustom, calls=%fused_computation.154 | custom fusion | bytes 1540 | tf_op jit(solution)/shard_map/scatter | solution.py:96
  51.6 5.6 %all-to-all-done = bf16[8,96,1280]{2,1,0:T(8,128)(2,1)} async-done(((bf16[8,96,1280]{2,1,0:T(8,128)(2,1)}), bf16[8,96,1280]{2,1,0:T(8,128)(2,1)}, u32[]{:S(2)}, u32[]{:S(2)}) %all-to-all-start) | async-done | bytes 1966112 | tf_op jit(solution)/shard_map/all_to_all | solution.py:102
  57.2 5.6 %gather_fusion.1 = bf16[384,1280]{1,0:T(8,128)(2,1)} fusion(bf16[768,1280]{1,0:T(8,128)(2,1)} %bitcast.6, s32[1024]{0:T(1024)S(1)} %pad_clamp_fusion), kind=kCustom, calls=%fused_computation.1 | custom fusion | bytes 1967616 | tf_op jit(solution)/shard_map/gather | solution.py:103
  62.8 1.5 fusion.16
  64.3 6.2 %convolution_convert_fusion = bf16[384,1920]{1,0:T(8,128)(2,1)} fusion(bf16[1280,1920]{0,1:T(8,128)(2,1)} %bitcast.255, bf16[384,1280]{1,0:T(8,128)(2,1)} %gather_fusion.1, f32[1280]{0:T(1024)S(1)} %copy-done.7, f32[384]{0:T(512)S(1)} %add_rsqrt_fusion.2), kind=kOutput, calls=%fused_computation.27 | convolution fusion | flops 1890140160 | bytes 7379456 | tf_op jit(solution)/shard_map/dot_general | solution.py:105
  70.5 2.6 copy.26
  73.0 3.9 copy.27
  77.0 4.5 all-to-all-start.1
  83.8 23.4 %all-to-all-done.1 = bf16[384,3,640]{0,1,2:T(4,128)(2,1)} async-done(((bf16[384,3,640]{0,1,2:T(4,128)(2,1)}), bf16[384,3,640]{0,1,2:T(4,128)(2,1)}, u32[]{:S(2)}, u32[]{:S(2)}) %all-to-all-start.1) | async-done | bytes 1474592 | tf_op jit(solution)/shard_map/all_to_all | solution.py:109
  107.3 1.7 copy.28
  110.4 0.9 fusion.122
  111.4 1.4 fusion.123
  113.8 1.9 fusion.124
  116.5 2.3 fusion.125
  118.8 0.9 fusion.75
  119.8 2.7 fusion.126
  122.5 1.1 fusion.69
  123.6 12.4 %all_to_all.46 = bf16[8,384,80]{1,2,0:T(8,128)(2,1)S(1)} all-to-all(bf16[8,384,80]{1,2,0:T(8,128)(2,1)S(1)} %bitcast.258), channel_id=1, replica_groups=mesh['dp'=32,'seq'=8] {'seq'}, dimensions={0} | all-to-all | bytes 983040 | tf_op jit(solution)/shard_map/all_to_all | solution.py:155
  136.9 2.9 fusion.127
  139.7 54.4 %all-gather.3.cloned.1.call-done = bf16[256,5,640]{2,1,0:T(8,128)(2,1)} async-done(((bf16[1,5,640]{2,1,0:T(8,128)(2,1)}), bf16[256,5,640]{2,1,0:T(8,128)(2,1)}) %all-gather.3.cloned.1.call-update) | async-done | bytes 1638416 | tf_op jit(solution)/shard_map/all_gather | solution.py:158
  194.1 4.1 reshape.456
  198.2 3.8 fusion.10
  202.0 262.3 %all-reduce.4.cloned.1.call-done = f32[640,1280]{0,1:T(8,128)} async-done(((f32[640,1280]{0,1:T(8,128)}), f32[640,1280]{0,1:T(8,128)}) %all-reduce.4.cloned.1.call-update) | async-done | bytes 3276816
  464.3 1.4 constant_dynamic-slice_fusion
  (60 shorter events, 7.9 us)
Async XLA Ops:
  7.2 5.9 %copy-start = (bf16[1280,1280]{1,0:T(8,128)(2,1)S(1)}, bf16[1280,1280]{1,0:T(8,128)(2,1)}, u32[]{:S(2)}) copy-start(bf16[1280,1280]{1,0:T(8,128)(2,1)} %param.19) | copy-start | bytes 9830404
  13.1 4.2 copy-start.4
  13.1 4.2 copy-start.5
  13.1 4.2 copy-start.6
  26.8 30.4 %all-to-all-start = ((bf16[8,96,1280]{2,1,0:T(8,128)(2,1)}), bf16[8,96,1280]{2,1,0:T(8,128)(2,1)}, u32[]{:S(2)}, u32[]{:S(2)}) async-start(bf16[8,96,1280]{2,1,0:T(8,128)(2,1)} %bitcast.252), calls=%async_computation | async-start | bytes 3932160 | tf_op jit(solution)/shard_map/all_to_all | solution.py:102
  57.2 7.1 %copy-start.7 = (f32[1280]{0:T(1024)S(1)}, f32[1280]{0:T(1024)}, u32[]{:S(2)}) copy-start(f32[1280]{0:T(1024)} %param.21) | copy-start | bytes 15364
  76.9 5.5 %copy-start.8 = (f32[8]{0:T(128)S(1)}, f32[8]{0:T(128)}, u32[]{:S(2)}) copy-start(f32[8]{0:T(128)} %param.22) | copy-start | bytes 100
  76.9 6.8 %copy-start.3 = (s32[1,3072]{1,0:T(1,128)S(1)}, s32[1,3072]{1,0:T(1,128)}, u32[]{:S(2)}) copy-start(s32[1,3072]{1,0:T(1,128)} %param.14) | copy-start | bytes 36868
  77.0 30.3 %all-to-all-start.1 = ((bf16[384,3,640]{0,1,2:T(4,128)(2,1)}), bf16[384,3,640]{0,1,2:T(4,128)(2,1)}, u32[]{:S(2)}, u32[]{:S(2)}) async-start(bf16[384,3,640]{0,1,2:T(4,128)(2,1)} %copy.27), calls=%async_computation.1 | async-start | bytes 3932160 | tf_op jit(solution)/shard_map/all_to_all | solution.py:109
  81.4 112.7 %all-gather.3.cloned.1.call-start = ((), (), s32[]{:S(2)}) async-start(), calls=%async_computation.3 | async-start | bytes 2631680 | tf_op jit(solution)/shard_map/all_gather | solution.py:158
  82.2 382.1 %all-reduce.4.cloned.1.call-start = ((), (), s32[]{:S(2)}) async-start(), calls=%async_computation.4 | async-start | bytes 6553600
  109.7 0.7 slice-start
  112.7 1.1 slice-start.1
  122.5 14.4 %copy-start.2 = (bf16[384,1280]{1,0:T(8,128)(2,1)S(1)}, bf16[384,1280]{1,0:T(8,128)(2,1)}, u32[]{:S(2)}) copy-start(bf16[384,1280]{1,0:T(8,128)(2,1)} %param.25) | copy-start | bytes 2949124
  136.1 0.8 copy-start.1
Sparse Core Ops, SparseCore 0:
  86.0 108.0 all-gather.2
  199.6 264.6 all-reduce.3
where the time goes:
time: 474 us; the launch traced here: 473 us
  waiting for transfers between devices  346 us (73%)
  local copies, waits for them, and re-layouts  52.6 us (11%)
  matrix products  32.7 us (7%)
  between operations  15 us (3%)
  blocking collectives  12.4 us (3%)
  starting transfers between devices  9.23 us (2%)
    unnamed x3, waiting for transfers between devices  263 us
    all_gather x1, waiting for transfers between devices, per_device(): lax.all_gather(out_weight, ('dp', 'seq'), axis=1, tiled=True)  54.4 us
    all_to_all x1, waiting for transfers between devices, per_device(): lax.all_to_all(projected, 'seq', split_axis=2, concat_axis=0, tiled=True)  23.4 us
    unnamed x21, local copies, waits for them, and re-layouts  14.5 us
    all_to_all x1, blocking collectives, per_device(): lax.all_to_all(attended, 'seq', split_axis=0, concat_axis=1, tiled=True)  12.4 us
    scatter x1, local copies, waits for them, and re-layouts, per_device(): receive_table = jnp.zeros((shard_rows,), jnp.int32).at[landing].set(loade...  11.9 us
    dot_general x6, matrix products, per_device(): jnp.einsum('qhd,khd->hqk', query_part, key_part, preferred_element_type=j...  9.69 us
  transfers between devices with their start and end apart: 4, of which 4 were waited for; matrix products, arithmetic and copies ran while one was open for 10% of the time, Pallas kernels for 0%

commit v1 on v0

--- a/solution.py
+++ b/solution.py
@@ -7,6 +7,30 @@
 HD = 80
 EPSILON = 1e-06
 CONTRACT_FIRST = (((0,), (0,)), ((), ()))
+
+
+def in_blocks(shard, dim, length):
+    shape = shard.shape
+    blocks = shard.reshape(*shape[:dim], length, shape[dim] // length, *shape[dim + 1 :])
+    return jnp.moveaxis(blocks, dim, 0)
+
+
+def in_order(pieces, dim):
+    dims = list(pieces.shape[1:])
+    dims[dim] *= pieces.shape[0]
+    return jnp.moveaxis(pieces, 0, dim).reshape(dims)
+
+
+def rotated_exchange(x, axis, split_dim, concat_dim):
+    size, mine = (lax.axis_size(axis), lax.axis_index(axis))
+    blocks = in_blocks(x, split_dim, size)
+    result = blocks
+    for step in range(1, size):
+        target, source = ((mine + step) % size, (mine - step) % size)
+        sent = lax.dynamic_index_in_dim(blocks, target, 0)
+        partner_block = lax.ppermute(sent, axis, [(i, (i + step) % size) for i in range(size)])
+        result = lax.dynamic_update_slice_in_dim(result, partner_block, source, axis=0)
+    return in_order(result, concat_dim)
 
 
 def row_norm(values):
@@ -106,7 +130,7 @@
         normed, qkv_weight.reshape(model_width, -1), preferred_element_type=jnp.float32
     )
     projected = projected.astype(jnp.bfloat16).reshape(shard_rows, 3, -1)
-    head_rows = lax.all_to_all(projected, "seq", split_axis=2, concat_axis=0, tiled=True)
+    head_rows = rotated_exchange(projected, "seq", 2, 0)
     local_width = head_rows.shape[2]
     local_heads = local_width // HD
     queries = row_norm(

time: 474 us -> 427 us (0.901)
  waiting for transfers between devices: 346 us -> 299 us
    all_gather x1, waiting for transfers between devices: 54.4 us -> 20.3 us  [per_device(): lax.all_gather(out_weight, ('dp', 'seq'), axis=1, tiled=True)]
    all_to_all x1 -> x0, waiting for transfers between devices: 23.4 us -> none  [per_device(): lax.all_to_all(projected, 'seq', split_axis=2, concat_axis=0, tiled=True)]
    ppermute x0 -> x7, waiting for transfers between devices: none -> 12.4 us  [rotated_exchange(): lax.ppermute(sent, axis, [(i, (i + step) % size) for i in range(size)])]
    ppermute x0 -> x7, starting transfers between devices: none -> 7.83 us  [rotated_exchange(): lax.ppermute(sent, axis, [(i, (i + step) % size) for i in range(size)])]
    unnamed x21 -> x23, local copies, waits for them, and re-layouts: 14.5 us -> 14.6 us
  transfers between devices with their start and end apart: 4 -> 10, of which waited for: 4 -> 10; matrix products, arithmetic and copies ran while one was open for 10% -> 15% of each run, Pallas kernels for 0% -> 0%
where the time goes in v1:
time: 427 us
  waiting for transfers between devices  299 us (70%)
  local copies, waits for them, and re-layouts  48.6 us (11%)
  matrix products  32.7 us (8%)
  between operations  15.4 us (4%)
  blocking collectives  14.3 us (3%)
  starting transfers between devices  12.4 us (3%)
    unnamed x3, waiting for transfers between devices  263 us
    all_gather x1, waiting for transfers between devices, per_device(): lax.all_gather(out_weight, ('dp', 'seq'), axis=1, tiled=True)  20.3 us
    unnamed x23, local copies, waits for them, and re-layouts  14.6 us
    all_to_all x1, blocking collectives, per_device(): lax.all_to_all(attended, 'seq', split_axis=0, concat_axis=1, tiled=True)  14.3 us
    ppermute x7, waiting for transfers between devices, rotated_exchange(): lax.ppermute(sent, axis, [(i, (i + step) % size) for i in range(size)])  12.4 us
    scatter x1, local copies, waits for them, and re-layouts, per_device(): receive_table = jnp.zeros((shard_rows,), jnp.int32).at[landing].set(loade...  11.8 us
    dot_general x6, matrix products, per_device(): jnp.einsum('qhd,khd->hqk', query_part, key_part, preferred_element_type=j...  9.7 us
  transfers between devices with their start and end apart: 10, of which 10 were waited for; matrix products, arithmetic and copies ran while one was open for 15% of the time, Pallas kernels for 0%

profile of v1, /device:TPU:2, one launch (start us, length us, event | category | flops | bytes accessed | tf_op | source)
XLA Modules:
  0.0 426.6 jit_solution(8471343492828350736)
XLA Ops:
  10.1 2.9 scatter_custom_fusion
  13.1 4.2 fusion.23
  17.3 2.0 fusion.9
  20.3 6.5 %gather_fusion = bf16[768,1280]{1,0:T(8,128)(2,1)} fusion(bf16[385,1280]{1,0:T(8,128)(2,1)} %concatenate.7, s32[1024]{0:T(1024)S(1)} %pad_clamp_fusion.1), kind=kCustom, calls=%fused_computation | custom fusion | bytes 3935232 | tf_op jit(solution)/shard_map/gather | solution.py:126
  26.8 4.5 %all-to-all-start = ((bf16[8,96,1280]{2,1,0:T(8,128)(2,1)}), bf16[8,96,1280]{2,1,0:T(8,128)(2,1)}, u32[]{:S(2)}, u32[]{:S(2)}) async-start(bf16[8,96,1280]{2,1,0:T(8,128)(2,1)} %bitcast.268), calls=%async_computation | async-start | bytes 3932160 | tf_op jit(solution)/shard_map/all_to_all | solution.py:126
  32.4 8.2 %copy.23 = bf16[1280,3,640]{0,2,1:T(8,128)(2,1)} copy(bf16[1280,3,640]{2,0,1:T(8,128)(2,1)} %param.23) | data formatting | bytes 9830400 | tf_op args[10]
  41.9 11.8 %scatter_custom_fusion.1 = s32[384]{0:T(512)S(1)} fusion(s32[3072]{0:T(1024)S(1)} %bitcast.279, s32[3072]{0:T(1024)S(1)} %get-tuple-element.43, s32[]{:T(128)} %constant.151.clone.1), kind=kCustom, calls=%fused_computation.168 | custom fusion | bytes 1540 | tf_op jit(solution)/shard_map/scatter | solution.py:120
  53.9 3.4 all-to-all-done
  57.3 5.6 %gather_fusion.1 = bf16[384,1280]{1,0:T(8,128)(2,1)} fusion(bf16[768,1280]{1,0:T(8,128)(2,1)} %bitcast.6, s32[1024]{0:T(1024)S(1)} %pad_clamp_fusion), kind=kCustom, calls=%fused_computation.1 | custom fusion | bytes 1967616 | tf_op jit(solution)/shard_map/gather | solution.py:127
  62.9 1.5 fusion.16
  64.3 6.1 %convolution_convert_fusion = bf16[384,1920]{1,0:T(8,128)(2,1)} fusion(bf16[1280,1920]{0,1:T(8,128)(2,1)} %bitcast.269, bf16[384,1280]{1,0:T(8,128)(2,1)} %gather_fusion.1, f32[1280]{0:T(1024)S(1)} %copy-done.8, f32[384]{0:T(512)S(1)} %add_rsqrt_fusion.2), kind=kOutput, calls=%fused_computation.27 | convolution fusion | flops 1890140160 | bytes 7379456 | tf_op jit(solution)/shard_map/dot_general | solution.py:129
  70.5 2.6 copy.24
  73.0 1.6 dynamic-slice_bitcast_fusion
  75.5 1.2 collective-permute-start.2
  76.7 2.7 collective-permute-start.3
  80.5 1.4 collective-permute-done
  82.0 1.6 collective-permute-done.1
  83.6 2.0 collective-permute-start.6
  85.6 3.9 collective-permute-done.2
  89.6 1.7 collective-permute-done.3
  92.9 2.2 collective-permute-done.6
  97.5 1.4 fusion.123
  99.9 1.9 fusion.124
  102.7 2.3 fusion.125
  105.9 2.7 fusion.126
  109.8 14.3 %all_to_all.28 = bf16[8,384,80]{1,2,0:T(8,128)(2,1)S(1)} all-to-all(bf16[8,384,80]{1,2,0:T(8,128)(2,1)S(1)} %bitcast.272), channel_id=1, replica_groups=mesh['dp'=32,'seq'=8] {'seq'}, dimensions={0} | all-to-all | bytes 983040 | tf_op jit(solution)/shard_map/all_to_all | solution.py:179
  124.8 2.9 fusion.127
  127.8 20.3 %all-gather.3.cloned.1.call-done = bf16[256,5,640]{2,1,0:T(8,128)(2,1)} async-done(((bf16[1,5,640]{2,1,0:T(8,128)(2,1)}), bf16[256,5,640]{2,1,0:T(8,128)(2,1)}) %all-gather.3.cloned.1.call-update) | async-done | bytes 1638416 | tf_op jit(solution)/shard_map/all_gather | solution.py:182
  148.0 4.1 reshape.463
  152.1 3.8 fusion.10
  155.9 262.5 %all-reduce.4.cloned.1.call-done = f32[640,1280]{0,1:T(8,128)} async-done(((f32[640,1280]{0,1:T(8,128)}), f32[640,1280]{0,1:T(8,128)}) %all-reduce.4.cloned.1.call-update) | async-done | bytes 3276816
  418.4 1.4 constant_dynamic-slice_fusion
  (80 shorter events, 16.2 us)
Async XLA Ops:
  7.2 5.9 %copy-start = (bf16[1280,1280]{1,0:T(8,128)(2,1)S(1)}, bf16[1280,1280]{1,0:T(8,128)(2,1)}, u32[]{:S(2)}) copy-start(bf16[1280,1280]{1,0:T(8,128)(2,1)} %param.19) | copy-start | bytes 9830404
  13.1 4.2 copy-start.5
  13.1 4.2 copy-start.6
  13.1 4.2 copy-start.7
  26.8 30.4 %all-to-all-start = ((bf16[8,96,1280]{2,1,0:T(8,128)(2,1)}), bf16[8,96,1280]{2,1,0:T(8,128)(2,1)}, u32[]{:S(2)}, u32[]{:S(2)}) async-start(bf16[8,96,1280]{2,1,0:T(8,128)(2,1)} %bitcast.268), calls=%async_computation | async-start | bytes 3932160 | tf_op jit(solution)/shard_map/all_to_all | solution.py:126
  31.3 116.7 %all-gather.3.cloned.1.call-start = ((), (), s32[]{:S(2)}) async-start(), calls=%async_computation.2 | async-start | bytes 2631680 | tf_op jit(solution)/shard_map/all_gather | solution.py:182
  32.0 386.3 %all-reduce.4.cloned.1.call-start = ((), (), s32[]{:S(2)}) async-start(), calls=%async_computation.3 | async-start | bytes 6553600
  32.4 8.2 %copy-start.9 = (f32[8]{0:T(128)S(1)}, f32[8]{0:T(128)}, u32[]{:S(2)}) copy-start(f32[8]{0:T(128)} %param.22) | copy-start | bytes 100
  32.4 21.4 %copy-start.4 = (s32[1,3072]{1,0:T(1,128)S(1)}, s32[1,3072]{1,0:T(1,128)}, u32[]{:S(2)}) copy-start(s32[1,3072]{1,0:T(1,128)} %param.14) | copy-start | bytes 36868
  57.2 7.1 %copy-start.8 = (f32[1280]{0:T(1024)S(1)}, f32[1280]{0:T(1024)}, u32[]{:S(2)}) copy-start(f32[1280]{0:T(1024)} %param.21) | copy-start | bytes 15364
  73.0 8.9 %copy-start.1 = (bf16[384,1920]{0,1:T(8,128)(2,1)S(1)}, bf16[384,1920]{0,1:T(8,128)(2,1)}, u32[]{:S(2)}) copy-start(bf16[384,1920]{0,1:T(8,128)(2,1)} %copy.24) | copy-start | bytes 4423684
  74.6 7.3 %collective-permute-start = (bf16[1,384,3,80]{1,3,0,2:T(8,128)(2,1)S(1)}, bf16[1,384,3,80]{1,3,0,2:T(8,128)(2,1)S(1)}, u32[]{:S(2)}, u32[]{:S(2)}) collective-permute-start(bf16[1,384,3,80]{1,3,0,2:T(8,128)(2,1)S(1)} %get-tuple-element.16), channel_id=1, source_target_pairs={{0,1},{1,2},{2,3},{3,4},{4,5},{5,6},{6,7},{7,0},{8,9},{9,10},{10,1... | collective-permute-start | bytes 552968 | tf_op jit(solution)/shard_map/ppermute | solution.py:31
  74.7 9.0 %collective-permute-start.1 = (bf16[1,384,3,80]{1,3,0,2:T(8,128)(2,1)S(1)}, bf16[1,384,3,80]{1,3,0,2:T(8,128)(2,1)S(1)}, u32[]{:S(2)}, u32[]{:S(2)}) collective-permute-start(bf16[1,384,3,80]{1,3,0,2:T(8,128)(2,1)S(1)} %get-tuple-element.15), channel_id=1, source_target_pairs={{0,2},{1,3},{2,4},{3,5},{4,6},{5,7},{6,0},{7,1},{8,10},{9,11},{10,... | collective-permute-start | bytes 552968 | tf_op jit(solution)/shard_map/ppermute | solution.py:31
  75.5 14.0 %collective-permute-start.2 = (bf16[1,384,3,80]{1,3,0,2:T(8,128)(2,1)S(1)}, bf16[1,384,3,80]{1,3,0,2:T(8,128)(2,1)S(1)}, u32[]{:S(2)}, u32[]{:S(2)}) collective-permute-start(bf16[1,384,3,80]{1,3,0,2:T(8,128)(2,1)S(1)} %get-tuple-element.14), channel_id=1, source_target_pairs={{0,3},{1,4},{2,5},{3,6},{4,7},{5,0},{6,1},{7,2},{8,11},{9,12},{10,... | collective-permute-start | bytes 552968 | tf_op jit(solution)/shard_map/ppermute | solution.py:31
  76.7 14.6 %collective-permute-start.3 = (bf16[1,384,3,80]{1,3,0,2:T(8,128)(2,1)S(1)}, bf16[1,384,3,80]{1,3,0,2:T(8,128)(2,1)S(1)}, u32[]{:S(2)}, u32[]{:S(2)}) collective-permute-start(bf16[1,384,3,80]{1,3,0,2:T(8,128)(2,1)S(1)} %get-tuple-element.13), channel_id=1, source_target_pairs={{0,4},{1,5},{2,6},{3,7},{4,0},{5,1},{6,2},{7,3},{8,12},{9,13},{10,... | collective-permute-start | bytes 552968 | tf_op jit(solution)/shard_map/ppermute | solution.py:31
  79.4 12.3 %collective-permute-start.4 = (bf16[1,384,3,80]{1,3,0,2:T(8,128)(2,1)S(1)}, bf16[1,384,3,80]{1,3,0,2:T(8,128)(2,1)S(1)}, u32[]{:S(2)}, u32[]{:S(2)}) collective-permute-start(bf16[1,384,3,80]{1,3,0,2:T(8,128)(2,1)S(1)} %get-tuple-element.12), channel_id=1, source_target_pairs={{0,5},{1,6},{2,7},{3,0},{4,1},{5,2},{6,3},{7,4},{8,13},{9,14},{10,... | collective-permute-start | bytes 552968 | tf_op jit(solution)/shard_map/ppermute | solution.py:31
  82.0 10.9 %collective-permute-start.5 = (bf16[1,384,3,80]{1,3,0,2:T(8,128)(2,1)S(1)}, bf16[1,384,3,80]{1,3,0,2:T(8,128)(2,1)S(1)}, u32[]{:S(2)}, u32[]{:S(2)}) collective-permute-start(bf16[1,384,3,80]{1,3,0,2:T(8,128)(2,1)S(1)} %get-tuple-element.11), channel_id=1, source_target_pairs={{0,6},{1,7},{2,0},{3,1},{4,2},{5,3},{6,4},{7,5},{8,14},{9,15},{10,... | collective-permute-start | bytes 552968 | tf_op jit(solution)/shard_map/ppermute | solution.py:31
  83.6 11.5 %collective-permute-start.6 = (bf16[1,384,3,80]{1,3,0,2:T(8,128)(2,1)S(1)}, bf16[1,384,3,80]{1,3,0,2:T(8,128)(2,1)S(1)}, u32[]{:S(2)}, u32[]{:S(2)}) collective-permute-start(bf16[1,384,3,80]{1,3,0,2:T(8,128)(2,1)S(1)} %get-tuple-element.10), channel_id=1, source_target_pairs={{0,7},{1,0},{2,1},{3,2},{4,3},{5,4},{6,5},{7,6},{8,15},{9,8},{10,9... | collective-permute-start | bytes 552968 | tf_op jit(solution)/shard_map/ppermute | solution.py:31
  95.9 0.7 slice-start
  98.9 1.1 slice-start.1
  108.6 16.2 %copy-start.3 = (bf16[384,1280]{1,0:T(8,128)(2,1)S(1)}, bf16[384,1280]{1,0:T(8,128)(2,1)}, u32[]{:S(2)}) copy-start(bf16[384,1280]{1,0:T(8,128)(2,1)} %param.25) | copy-start | bytes 2949124
  124.0 0.8 copy-start.2
Sparse Core Ops, SparseCore 0:
  35.9 112.1 all-gather.2
  153.5 264.8 all-reduce.3
